TPU v7x, 128 devices: a whole 4x4x4 slice. The times are simulated.
128 devices in a mesh: dp: 8 (over x, core), cent: 16 (over y, z).
Axes of the slice: x: 4, y: 4, z: 4, core: 2. Of those that a mesh axis runs over, the one named last changes fastest.
Arguments:
- vectors: bfloat16 [32768, 256], P(('dp', 'cent')), may hold values from -64 to 64
- owners: int32 [32768, 8], P(('dp', 'cent')), may hold values from 0 to 127, all different within a row; in each aligned block of 256 rows (0 to 255, 256 to 511, ...) at most 32 rows name the same one
- centroids: bfloat16 [262144, 256], P(('dp', 'cent')), may hold values from -6 to 6
- penalty: int32 [262144], P(('dp', 'cent')), may hold values from 0 to 7
Outputs:
- refined: float32 [262144, 256], P(('dp', 'cent'))
- energy: float32 [], replicated
Inputs may be any that keep to these rules, and one draw needn't show every extreme that they name: `owners`: each row names 8 different partitions; within the rows of one device no partition is named more than 32 times, a bound that some block reaches.
All inputs are finite; a program needn't handle non-finite values.
Results may differ from a plain program's by a relative error of at most 0.003.
Values may be sent and summed in bfloat16 or wider, within the bound.
A program may use at most 64 MiB of HBM per device.

v0:
```python
import math

import jax
import jax.numpy as jnp
from jax import lax
from jax.sharding import PartitionSpec as P

sharpness = 4.0
penalty_weight = 0.5
energy_scale = 16.0


def body(vectors, owners, centroids, penalty):
    row_count, feat_width = vectors.shape
    replicas = owners.shape[1]
    partitions = lax.axis_size(("dp", "cent"))
    capacity = 2 * row_count * replicas // partitions
    local_sq = jnp.sum(jnp.square(vectors.astype(jnp.float32)))
    total_sq = lax.psum(local_sq, ("dp", "cent"))
    score_scale = 1.0 / (sharpness * (total_sq / (row_count * partitions * feat_width)))
    targets = owners.reshape(-1)
    matches = (targets[:, None] == jnp.arange(partitions, dtype=jnp.int32)[None, :]).astype(
        jnp.int32
    )
    position = jnp.sum((jnp.cumsum(matches, axis=0) - matches) * matches, axis=1)
    source = jnp.arange(row_count * replicas, dtype=jnp.int32) // replicas
    outgoing = (
        jnp.zeros((partitions, capacity, feat_width), jnp.bfloat16)
        .at[targets, position]
        .set(vectors[source])
    )
    flags = jnp.zeros((partitions, capacity), jnp.bfloat16).at[targets, position].set(1.0)
    arrived, arrived_flags = (
        lax.all_to_all(outgoing, ("dp", "cent"), split_axis=0, concat_axis=0, tiled=True),
        lax.all_to_all(flags, ("dp", "cent"), split_axis=0, concat_axis=0, tiled=True),
    )
    slot_total_count = partitions * capacity
    block_rows = math.gcd(slot_total_count, 512)
    block_count = slot_total_count // block_rows
    arrived_rows = arrived.reshape(slot_total_count, feat_width)
    arrived_live = arrived_flags.reshape(slot_total_count).astype(jnp.float32)
    cent_norms = jnp.sum(jnp.square(centroids.astype(jnp.float32)), axis=1)
    offsets = penalty_weight * penalty.astype(jnp.float32)

    def logits_for(row_block):
        products = lax.dot_general(
            row_block, centroids, (((1,), (1,)), ((), ())), preferred_element_type=jnp.float32
        )
        row_norms = jnp.sum(jnp.square(row_block.astype(jnp.float32)), axis=1)
        return (
            -(row_norms[:, None] - 2.0 * products + cent_norms[None, :]) * score_scale
            - offsets[None, :]
        )

    def partial_stats(row_block):
        logits = logits_for(row_block)
        peak_val = jnp.max(logits, axis=1)
        return (peak_val, jnp.sum(jnp.exp(logits - peak_val[:, None]), axis=1))

    def block_weights(row_block, norm_rows, live_rows):
        return (jnp.exp(logits_for(row_block) - norm_rows[:, None]) * live_rows[:, None]).astype(
            jnp.bfloat16
        )

    start_state = (
        jnp.zeros(centroids.shape, jnp.float32),
        jnp.zeros((centroids.shape[0],), jnp.float32),
    )
    blocks = arrived_rows.reshape(block_count, block_rows, feat_width)
    block_peaks, block_totals = lax.map(partial_stats, blocks)
    flat_peak = block_peaks.reshape(-1)
    flat_total = block_totals.reshape(-1)
    back_peak, back_total = (
        lax.all_to_all(
            flat_peak.reshape(partitions, capacity),
            ("dp", "cent"),
            split_axis=0,
            concat_axis=0,
            tiled=True,
        ),
        lax.all_to_all(
            flat_total.reshape(partitions, capacity),
            ("dp", "cent"),
            split_axis=0,
            concat_axis=0,
            tiled=True,
        ),
    )
    slot_peak = back_peak[targets, position].reshape(row_count, replicas)
    slot_total = back_total[targets, position].reshape(row_count, replicas)
    row_peak = jnp.max(slot_peak, axis=1)
    log_norm = row_peak + jnp.log(
        jnp.sum(slot_total * jnp.exp(slot_peak - row_peak[:, None]), axis=1)
    )
    norm_send = (
        jnp.zeros((partitions, capacity), jnp.float32)
        .at[targets, position]
        .set(jnp.repeat(log_norm, replicas))
    )
    norm_flat = lax.all_to_all(
        norm_send, ("dp", "cent"), split_axis=0, concat_axis=0, tiled=True
    ).reshape(slot_total_count)

    def accumulate(running, inputs):
        numerator, weight_sum = running
        row_block, norm_rows, live_rows = inputs
        weights = block_weights(row_block, norm_rows, live_rows)
        numerator = numerator + lax.dot_general(
            weights, row_block, (((0,), (0,)), ((), ())), preferred_element_type=jnp.float32
        )
        weight_sum = weight_sum + jnp.sum(weights.astype(jnp.float32), axis=0)
        return ((numerator, weight_sum), None)

    (numerator, weight_sum), unused = lax.scan(
        accumulate,
        start_state,
        (
            blocks,
            norm_flat.reshape(block_count, block_rows),
            arrived_live.reshape(block_count, block_rows),
        ),
    )
    refined = (centroids.astype(jnp.float32) + numerator) / (1.0 + weight_sum[:, None])
    norm_total = lax.psum(jnp.sum(log_norm), ("dp", "cent"))
    energy = -norm_total / (energy_scale * row_count * partitions)
    return (refined, energy)


def solution(mesh):
    placed = (
        P(("dp", "cent"), None),
        P(("dp", "cent"), None),
        P(("dp", "cent"), None),
        P(("dp", "cent")),
    )
    return jax.shard_map(
        body, mesh=mesh, in_specs=placed, out_specs=(P(("dp", "cent"), None), P()), check_vma=False
    )
```

profile of v0, /device:TPU:1, one launch (start us, length us, event | category | flops | bytes accessed | tf_op | source)
XLA Modules:
  0.0 368.6 jit_solution(4518713572303771877)
XLA Ops:
  3.7 17.3 %scatter_custom_fusion = bf16[4096,256]{1,0:T(8,128)(2,1)} fusion(s32[2048]{0:T(1024)S(1)} %get-tuple-element.185, bf16[256,256]{1,0:T(8,128)(2,1)S(1)} %copy-done.2, s32[2048]{0:T(1024)S(1)} %get-tuple-element.186, bf16[]{:T(256)} %constant.49.clone.1), kind=kCustom, calls=%fused_computation.32 | custom fusion | bytes 2097154
  21.1 11.5 %all-to-all-start = ((bf16[128,32,256]{2,1,0:T(8,128)(2,1)}), bf16[128,32,256]{2,1,0:T(8,128)(2,1)S(1)}, u32[]{:S(2)}, u32[]{:S(2)}) async-start(bf16[128,32,256]{2,1,0:T(8,128)(2,1)} %bitcast.79), calls=%async_computation | async-start | bytes 4194304 | tf_op jit(solution)/shard_map/all_to_all | solution.py:34
  33.2 81.2 %psum.14 = f32[]{:T(128)} all-reduce(f32[]{:T(128)} %multiply_reduce_fusion.2), channel_id=1, replica_groups=mesh['dp'=8,'cent'=16] {'dp','cent'}, use_global_device_ids=true, to_apply=%region_6.7 | all-reduce | flops 1 | bytes 8 | tf_op jit(solution)/shard_map/psum | solution.py:19
  115.6 19.0 %while.25 = (s32[]{:T(128)}, f32[8,512]{1,0:T(8,128)S(1)}, f32[8,512]{1,0:T(8,128)S(1)}, bf16[8,512,256]{2,1,0:T(8,128)(2,1)S(1)}, bf16[2048,256]{1,0:T(8,128)(2...) while((s32[]{:T(128)}, f32[8,512]{1,0:T(8,128)S(1)}, ...), condition=%wide.region_11.12_spmd, body=%wide.region_7.11_spmd.sunk | while | flops 546699776 | bytes 9996409 | solution.py:70
  135.5 5.9 %all-to-all-start.2 = ((f32[128,1,32]{2,1,0:T(1,128)}), f32[128,1,32]{2,1,0:T(1,128)S(1)}, u32[]{:S(2)}, u32[]{:S(2)}) async-start(f32[128,1,32]{2,1,0:T(1,128)} %bitcast.13), calls=%async_computation.2 | async-start | bytes 131072 | tf_op jit(solution)/shard_map/all_to_all | solution.py:81
  142.0 8.9 %all-to-all-done.2 = f32[128,1,32]{2,1,0:T(1,128)S(1)} async-done(((f32[128,1,32]{2,1,0:T(1,128)}), f32[128,1,32]{2,1,0:T(1,128)S(1)}, u32[]{:S(2)}, u32[]{:S(2)}) %all-to-all-start.2) | async-done | bytes 16416 | tf_op jit(solution)/shard_map/all_to_all | solution.py:81
  150.9 4.5 %all-to-all-start.1 = ((f32[128,1,32]{2,1,0:T(1,128)}), f32[128,1,32]{2,1,0:T(1,128)S(1)}, u32[]{:S(2)}, u32[]{:S(2)}) async-start(f32[128,1,32]{2,1,0:T(1,128)} %bitcast.10), calls=%async_computation.1 | async-start | bytes 131072 | tf_op jit(solution)/shard_map/all_to_all | solution.py:74
  155.5 14.6 %scatter_custom_fusion.2 = bf16[4096]{0:T(1024)(128)(2,1)S(1)} fusion(s32[2048]{0:T(1024)S(1)} %get-tuple-element.184, bf16[2048]{0:T(1024)(128)(2,1)S(1)} %broadcast.187, bf16[]{:T(256)} %constant.49.clone.1), kind=kCustom, calls=%fused_computation.61 | custom fusion | bytes 8194
  170.8 13.6 %gather_fusion.1 = f32[2048]{0:T(1024)S(1)} fusion(f32[128,32]{1,0:T(8,128)S(1)} %bitcast.75, s32[2048]{0:T(1024)S(1)} %bitcast.76), kind=kCustom, calls=%fused_computation.2 | custom fusion | bytes 32768 | tf_op jit(solution)/shard_map/gather | solution.py:90
  184.6 9.9 %all-to-all-start.4 = ((bf16[128,1,32]{2,1,0:T(2,128)(2,1)}), bf16[128,1,32]{2,1,0:T(2,128)(2,1)S(1)}, u32[]{:S(2)}, u32[]{:S(2)}) async-start(bf16[128,1,32]{2,1,0:T(2,128)(2,1)} %copy.21), calls=%async_computation.4 | async-start | bytes 131072 | tf_op jit(solution)/shard_map/all_to_all | solution.py:35
  194.5 13.6 %gather_fusion = f32[2048]{0:T(1024)S(1)} fusion(f32[128,32]{1,0:T(8,128)S(1)} %bitcast.74, s32[2048]{0:T(1024)S(1)} %bitcast.77), kind=kCustom, calls=%fused_computation.1 | custom fusion | bytes 32768 | tf_op jit(solution)/shard_map/gather | solution.py:89
  209.3 8.1 %scatter_custom_fusion.1 = f32[4096]{0:T(1024)S(1)} fusion(s32[2048]{0:T(1024)S(1)} %get-tuple-element.184, f32[2048]{0:T(1024)S(1)} %reshape.194, f32[]{:T(128)} %constant.44.clone.1), kind=kCustom, calls=%fused_computation.57 | custom fusion | bytes 16388
  218.1 9.8 %all-to-all-start.3 = ((f32[128,1,32]{2,1,0:T(1,128)}), f32[128,1,32]{2,1,0:T(1,128)S(1)}, u32[]{:S(2)}, u32[]{:S(2)}) async-start(f32[128,1,32]{2,1,0:T(1,128)} %copy.20), calls=%async_computation.3 | async-start | bytes 131072 | tf_op jit(solution)/shard_map/all_to_all | solution.py:100
  228.2 67.5 %psum.15 = f32[]{:T(128)} all-reduce(f32[]{:T(128)} %get-tuple-element.173), channel_id=1, replica_groups=mesh['dp'=8,'cent'=16] {'dp','cent'}, use_global_device_ids=true, to_apply=%region_21.22 | all-reduce | flops 1 | bytes 8 | tf_op jit(solution)/shard_map/psum | solution.py:124
  297.8 67.9 %while.26 = (s32[]{:T(128)}, f32[2048,256]{1,0:T(8,128)S(1)}, f32[2048]{0:T(1024)S(1)}, bf16[8,512,256]{2,1,0:T(8,128)(2,1)}, bf16[2048,256]{1,0:T(8,128)(2,1)S(...) while((s32[]{:T(128)}, f32[2048,256]{1,0:T(8,128)S(1)}, ...), condition=%wide.region_19.20_spmd.clone, body=%wide.region_16.19_spmd.clone.sunk | while | flops 1086719488 | bytes 10290824 | solution.py:114
  299.0 4.2 %convert_reduce_fusion.3 = (f32[2048]{0:T(1024)S(1)}, bf16[512,2048]{1,0:T(8,128)(2,1)}) fusion(f32[512]{0:T(512)S(1)} %bitcast.83, f32[512]{0:T(512)S(1)} %bitcast.84, f32[2048]{0:T(1024)S(1)} %get-tuple-element.370, f32[]{:T(128)} %get-tuple-element.369, f32[2048]{0:T(1024)S(1)} %get-tuple-element.368, ...), kind=kOutput, calls=%fused_computation.12.clone.1 | convolution fusion | flops 548403200 | bytes 3439616 | tf_op jit(solution)/shard_map/while/body/eval_jaxpr/dot_general | solution.py:46
  303.2 3.2 convolution_add_fusion.2
  307.5 4.2 %convert_reduce_fusion.3 = (f32[2048]{0:T(1024)S(1)}, bf16[512,2048]{1,0:T(8,128)(2,1)}) fusion(f32[512]{0:T(512)S(1)} %bitcast.83, f32[512]{0:T(512)S(1)} %bitcast.84, f32[2048]{0:T(1024)S(1)} %get-tuple-element.370, f32[]{:T(128)} %get-tuple-element.369, f32[2048]{0:T(1024)S(1)} %get-tuple-element.368, ...), kind=kOutput, calls=%fused_computation.12.clone.1 | convolution fusion | flops 548403200 | bytes 3439616 | tf_op jit(solution)/shard_map/while/body/eval_jaxpr/dot_general | solution.py:46
  311.6 3.2 convolution_add_fusion.2
  316.0 4.2 %convert_reduce_fusion.3 = (f32[2048]{0:T(1024)S(1)}, bf16[512,2048]{1,0:T(8,128)(2,1)}) fusion(f32[512]{0:T(512)S(1)} %bitcast.83, f32[512]{0:T(512)S(1)} %bitcast.84, f32[2048]{0:T(1024)S(1)} %get-tuple-element.370, f32[]{:T(128)} %get-tuple-element.369, f32[2048]{0:T(1024)S(1)} %get-tuple-element.368, ...), kind=kOutput, calls=%fused_computation.12.clone.1 | convolution fusion | flops 548403200 | bytes 3439616 | tf_op jit(solution)/shard_map/while/body/eval_jaxpr/dot_general | solution.py:46
  320.1 3.2 convolution_add_fusion.2
  324.5 4.2 %convert_reduce_fusion.3 = (f32[2048]{0:T(1024)S(1)}, bf16[512,2048]{1,0:T(8,128)(2,1)}) fusion(f32[512]{0:T(512)S(1)} %bitcast.83, f32[512]{0:T(512)S(1)} %bitcast.84, f32[2048]{0:T(1024)S(1)} %get-tuple-element.370, f32[]{:T(128)} %get-tuple-element.369, f32[2048]{0:T(1024)S(1)} %get-tuple-element.368, ...), kind=kOutput, calls=%fused_computation.12.clone.1 | convolution fusion | flops 548403200 | bytes 3439616 | tf_op jit(solution)/shard_map/while/body/eval_jaxpr/dot_general | solution.py:46
  328.6 3.2 convolution_add_fusion.2
  333.0 4.2 %convert_reduce_fusion.3 = (f32[2048]{0:T(1024)S(1)}, bf16[512,2048]{1,0:T(8,128)(2,1)}) fusion(f32[512]{0:T(512)S(1)} %bitcast.83, f32[512]{0:T(512)S(1)} %bitcast.84, f32[2048]{0:T(1024)S(1)} %get-tuple-element.370, f32[]{:T(128)} %get-tuple-element.369, f32[2048]{0:T(1024)S(1)} %get-tuple-element.368, ...), kind=kOutput, calls=%fused_computation.12.clone.1 | convolution fusion | flops 548403200 | bytes 3439616 | tf_op jit(solution)/shard_map/while/body/eval_jaxpr/dot_general | solution.py:46
  337.1 3.2 convolution_add_fusion.2
  341.4 4.2 %convert_reduce_fusion.3 = (f32[2048]{0:T(1024)S(1)}, bf16[512,2048]{1,0:T(8,128)(2,1)}) fusion(f32[512]{0:T(512)S(1)} %bitcast.83, f32[512]{0:T(512)S(1)} %bitcast.84, f32[2048]{0:T(1024)S(1)} %get-tuple-element.370, f32[]{:T(128)} %get-tuple-element.369, f32[2048]{0:T(1024)S(1)} %get-tuple-element.368, ...), kind=kOutput, calls=%fused_computation.12.clone.1 | convolution fusion | flops 548403200 | bytes 3439616 | tf_op jit(solution)/shard_map/while/body/eval_jaxpr/dot_general | solution.py:46
  345.6 3.2 convolution_add_fusion.2
  349.9 4.2 %convert_reduce_fusion.3 = (f32[2048]{0:T(1024)S(1)}, bf16[512,2048]{1,0:T(8,128)(2,1)}) fusion(f32[512]{0:T(512)S(1)} %bitcast.83, f32[512]{0:T(512)S(1)} %bitcast.84, f32[2048]{0:T(1024)S(1)} %get-tuple-element.370, f32[]{:T(128)} %get-tuple-element.369, f32[2048]{0:T(1024)S(1)} %get-tuple-element.368, ...), kind=kOutput, calls=%fused_computation.12.clone.1 | convolution fusion | flops 548403200 | bytes 3439616 | tf_op jit(solution)/shard_map/while/body/eval_jaxpr/dot_general | solution.py:46
  354.1 3.2 convolution_add_fusion.2
  358.4 4.2 %convert_reduce_fusion.3 = (f32[2048]{0:T(1024)S(1)}, bf16[512,2048]{1,0:T(8,128)(2,1)}) fusion(f32[512]{0:T(512)S(1)} %bitcast.83, f32[512]{0:T(512)S(1)} %bitcast.84, f32[2048]{0:T(1024)S(1)} %get-tuple-element.370, f32[]{:T(128)} %get-tuple-element.369, f32[2048]{0:T(1024)S(1)} %get-tuple-element.368, ...), kind=kOutput, calls=%fused_computation.12.clone.1 | convolution fusion | flops 548403200 | bytes 3439616 | tf_op jit(solution)/shard_map/while/body/eval_jaxpr/dot_general | solution.py:46
  362.6 3.2 convolution_add_fusion.2
  365.8 1.7 fusion.10
  (124 shorter events, 37.8 us)
Async XLA Ops:
  2.4 1.1 copy-start.6
  2.4 1.2 copy-start.4
  2.4 1.2 copy-start.5
  2.4 1.3 copy-start.2
  21.1 94.1 %copy-start.1 = (bf16[2048,256]{1,0:T(8,128)(2,1)S(1)}, bf16[2048,256]{1,0:T(8,128)(2,1)}, u32[]{:S(2)}) copy-start(bf16[2048,256]{1,0:T(8,128)(2,1)} %param.10) | copy-start | bytes 3145732
  21.1 94.5 %copy-start.3 = (s32[2048]{0:T(1024)S(1)}, s32[2048]{0:T(1024)}, u32[]{:S(2)}) copy-start(s32[2048]{0:T(1024)} %param.11) | copy-start | bytes 24580
  21.1 94.5 %all-to-all-start = ((bf16[128,32,256]{2,1,0:T(8,128)(2,1)}), bf16[128,32,256]{2,1,0:T(8,128)(2,1)S(1)}, u32[]{:S(2)}, u32[]{:S(2)}) async-start(bf16[128,32,256]{2,1,0:T(8,128)(2,1)} %bitcast.79), calls=%async_computation | async-start | bytes 4194304 | tf_op jit(solution)/shard_map/all_to_all | solution.py:34
  134.6 16.3 %copy-start = (bf16[8,512,256]{2,1,0:T(8,128)(2,1)}, bf16[8,512,256]{2,1,0:T(8,128)(2,1)S(1)}, u32[]{:S(2)}) copy-start(bf16[8,512,256]{2,1,0:T(8,128)(2,1)S(1)} %get-tuple-element.378) | copy-start | bytes 6291460
  135.5 15.5 %all-to-all-start.2 = ((f32[128,1,32]{2,1,0:T(1,128)}), f32[128,1,32]{2,1,0:T(1,128)S(1)}, u32[]{:S(2)}, u32[]{:S(2)}) async-start(f32[128,1,32]{2,1,0:T(1,128)} %bitcast.13), calls=%async_computation.2 | async-start | bytes 131072 | tf_op jit(solution)/shard_map/all_to_all | solution.py:81
  150.9 33.6 %all-to-all-start.1 = ((f32[128,1,32]{2,1,0:T(1,128)}), f32[128,1,32]{2,1,0:T(1,128)S(1)}, u32[]{:S(2)}, u32[]{:S(2)}) async-start(f32[128,1,32]{2,1,0:T(1,128)} %bitcast.10), calls=%async_computation.1 | async-start | bytes 131072 | tf_op jit(solution)/shard_map/all_to_all | solution.py:74
  184.6 33.6 %all-to-all-start.4 = ((bf16[128,1,32]{2,1,0:T(2,128)(2,1)}), bf16[128,1,32]{2,1,0:T(2,128)(2,1)S(1)}, u32[]{:S(2)}, u32[]{:S(2)}) async-start(bf16[128,1,32]{2,1,0:T(2,128)(2,1)} %copy.21), calls=%async_computation.4 | async-start | bytes 131072 | tf_op jit(solution)/shard_map/all_to_all | solution.py:35
  218.1 78.2 %all-to-all-start.3 = ((f32[128,1,32]{2,1,0:T(1,128)}), f32[128,1,32]{2,1,0:T(1,128)S(1)}, u32[]{:S(2)}, u32[]{:S(2)}) async-start(f32[128,1,32]{2,1,0:T(1,128)} %copy.20), calls=%async_computation.3 | async-start | bytes 131072 | tf_op jit(solution)/shard_map/all_to_all | solution.py:100
where the time goes:
time: 370 us; the launch traced here: 369 us
  blocking collectives  149 us (40%)
  local copies, waits for them, and re-layouts  74 us (20%)
  matrix products  69.5 us (19%)
  starting transfers between devices  41.6 us (11%)
  other arithmetic  21.8 us (6%)
  waiting for transfers between devices  8.89 us (2%)
    psum x1, blocking collectives, body(): total_sq = lax.psum(local_sq, ('dp', 'cent'))  81.2 us
    psum x1, blocking collectives, body(): norm_total = lax.psum(jnp.sum(log_norm), ('dp', 'cent'))  67.5 us
    dot_general x16, matrix products, logits_for(): lax.dot_general(row_block, centroids, (((1,), (1,)), ((), ())), preferred...  44.2 us
    unnamed x19, local copies, waits for them, and re-layouts  40.8 us
    dot_general x8, matrix products, accumulate(): lax.dot_general(weights, row_block, (((0,), (0,)), ((), ())), preferred_e...  25.3 us
    gather x1, local copies, waits for them, and re-layouts, body(): slot_peak = back_peak[targets, position].reshape(row_count, replicas)  13.6 us
    gather x1, local copies, waits for them, and re-layouts, body(): slot_total = back_total[targets, position].reshape(row_count, replicas)  13.6 us
    all_to_all x1, starting transfers between devices, body(): lax.all_to_all(outgoing, ('dp', 'cent'), split_axis=0, concat_axis=0, til...  11.5 us
  transfers between devices with their start and end apart: 5, of which 1 were waited for; matrix products, arithmetic and copies ran while one was open for 15% of the time, Pallas kernels for 0%

commit v1 on v0

v1 whole, which is shorter than its diff:
```python
import math

import jax
import jax.numpy as jnp
from jax import lax
from jax.experimental import pallas as pl
from jax.experimental.pallas import tpu as pltpu
from jax.sharding import PartitionSpec as P

sharpness = 4.0
penalty_weight = 0.5
energy_scale = 16.0

AXES = ("dp", "cent")
CAP = 32
DEAD = 3.0e38
LOG2E = math.log2(math.e)
LN2 = math.log(2.0)
MIB = 1024 * 1024

f32 = jnp.float32
bf16 = jnp.bfloat16
i32 = jnp.int32


def nt(a, b):
    return lax.dot_general(a, b, (((1,), (1,)), ((), ())), preferred_element_type=f32)


def iota(shape, axis):
    return lax.broadcasted_iota(i32, shape, axis)


def arrange(quarter, owners_t, vectors_ref, out_ref, rank_ref, src_ref):
    rows = vectors_ref.shape[0]
    parts = rank_ref.shape[0]
    part = iota((parts, rows), 0)
    match = part == owners_t[0:1, :]
    for r in range(1, owners_t.shape[0]):
        match = match | (part == owners_t[r : r + 1, :])
    before = jnp.where(iota((rows, rows), 0) < iota((rows, rows), 1), 1.0, 0.0).astype(bf16)
    rank = jnp.dot(jnp.where(match, 1.0, 0.0).astype(bf16), before, preferred_element_type=f32)
    rank_ref[...] = jnp.where(match, rank.astype(i32), -1)
    step = 8
    for g in range(parts // step):
        ranks = rank_ref[g * step : (g + 1) * step, :]
        hot = ranks[:, None, :] == iota((step, CAP, rows), 1)
        hot = jnp.where(hot, 1.0, 0.0).astype(bf16).reshape(step * CAP, rows)
        picked = jnp.dot(hot, vectors_ref[...], preferred_element_type=f32)
        out_ref[g * step * CAP : (g + 1) * step * CAP, :] = picked.astype(bf16)
    ranks = rank_ref[...]
    row = iota((parts, rows), 1)
    lane = iota((parts, 128), 1)
    src = jnp.full((parts, 128), -1, i32)
    for j in range(CAP):
        here = jnp.max(jnp.where(ranks == j, row, -1), axis=1, keepdims=True)
        src = jnp.where(lane == quarter * CAP + j, here, src)
    src_ref[...] = src


def fill_bias(mean_sq, centroids_ref, penalty_ref, bias_ref):
    n = centroids_ref.shape[0]
    eye = iota((128, 128), 0) == iota((128, 128), 1)
    for g in range(n // 128):
        c = centroids_ref[g * 128 : (g + 1) * 128, :].astype(f32)
        c = c * c
        half = sum(c[:, i : i + 128] for i in range(0, c.shape[1], 128)) * 0.5
        pen = penalty_ref[g : g + 1, :].astype(f32) * (penalty_weight * sharpness * 0.5 * mean_sq)
        col = jnp.sum(half + jnp.where(eye, pen, 0.0), axis=1, keepdims=True)
        bias_ref[g * 128 : (g + 1) * 128, :] = jnp.broadcast_to(col, (128, 128))


def wide(ref, rows, width):
    b = ref[rows, :]
    return jnp.concatenate([b] * (width // 128), axis=1)


def chunk_stats(factor, x, centroids_ref, bias_ref, u_ref, kb):
    n = centroids_ref.shape[0]
    width = x.shape[0]
    peak = jnp.full((8, width), -DEAD, f32)
    for k in range(0, n, kb):
        u = nt(centroids_ref[k : k + kb, :], x) - wide(bias_ref, pl.ds(k, kb), width)
        u_ref[k : k + kb, :] = u
        peak = jnp.maximum(peak, jnp.max(u.reshape(kb // 8, 8, width), axis=0))
    peak = jnp.max(peak, axis=0, keepdims=True)
    total = jnp.zeros((8, width), f32)
    for k in range(0, n, kb):
        p = jnp.exp2((u_ref[k : k + kb, :] - peak) * factor)
        total = total + jnp.sum(p.reshape(kb // 8, 8, width), axis=0)
    return peak * factor + jnp.log2(jnp.sum(total, axis=0, keepdims=True))


def home(quarter, scale, local_sq, lse, ranks_ref, src_ref):
    parts, rows = ranks_ref.shape
    logs = []
    for h in range(0, rows, 128):
        ranks = ranks_ref[:, h : h + 128]
        got = jnp.take_along_axis(lse, jnp.maximum(ranks, 0) + quarter * CAP, axis=1)
        got = jnp.where(ranks >= 0, got, -DEAD)
        peak = jnp.max(got, axis=0, keepdims=True)
        total = jnp.sum(jnp.where(ranks >= 0, jnp.exp2(got - peak), 0.0), axis=0, keepdims=True)
        logs.append(peak + jnp.log2(total))
    src = src_ref[...]
    norm = jnp.full((parts, 128), DEAD, f32)
    for h, log in enumerate(logs):
        got = jnp.take_along_axis(jnp.broadcast_to(log, (parts, 128)), jnp.bitwise_and(src, 127), axis=1)
        norm = jnp.where((src >= h * 128) & (src < (h + 1) * 128), got, norm)
    log_sum = LN2 * jnp.sum(sum(logs), axis=1, keepdims=True) - scale * local_sq
    spare = lax.rem(quarter + 1, 4) * CAP
    return jnp.where(iota((parts, 128), 1) == spare, log_sum, norm)


def arrange_kernel(owners_ref, vectors_ref, out_ref, rank_ref, src_ref):
    quarter = lax.rem(lax.axis_index("cent"), 4)
    arrange(quarter, owners_ref[...].T, vectors_ref, out_ref, rank_ref, src_ref)


def stats_kernel(mean_ref, x_ref, centroids_ref, penalty_ref, lse_ref, bias_ref, u_ref):
    mean_sq = mean_ref[0, 0]
    factor = LOG2E * 2.0 / (sharpness * mean_ref[0:1, :])
    factor = jnp.concatenate([factor, factor], axis=1)
    fill_bias(mean_sq, centroids_ref, penalty_ref, bias_ref)

    def chunk(t, _):
        x = x_ref[pl.ds(pl.multiple_of(t * 256, 256), 256), :]
        lse = chunk_stats(factor, x, centroids_ref, bias_ref, u_ref, 256)
        for half in range(2):
            row = lse[:, half * 128 : (half + 1) * 128]
            lse_ref[pl.ds(pl.multiple_of(t * 8 + half * 4, 4), 4)] = jnp.broadcast_to(row, (4, 1, 128))
        return 0

    lax.fori_loop(0, x_ref.shape[0] // 256, chunk, 0)


def home_kernel(mean_ref, sq_ref, lse_ref, rank_ref, src_ref, norm_ref):
    quarter = lax.rem(lax.axis_index("cent"), 4)
    lse = lse_ref[...].reshape(rank_ref.shape[0], 128)
    scale = 1.0 / (sharpness * mean_ref[0:1, 0:1])
    norm = home(quarter, scale, sq_ref[0:1, 0:1], lse, rank_ref, src_ref)
    norm_ref[...] = norm.reshape(norm_ref.shape)


def unpack_norms(norm, norm_ref):
    parts = norm.shape[0]
    lane = iota((parts, 128), 1)
    row = iota((parts, 128), 0)
    spare = lax.rem(lax.rem(row, 4) + 1, 4) * CAP
    log_sum = jnp.sum(jnp.where(lane == spare, norm, 0.0))
    mine = jnp.where(lane // CAP == lax.rem(row, 4), norm, 0.0)
    norm_ref[...] = jnp.sum(mine.reshape(parts // 4, 4, 128), axis=1)[:, None, :]
    return log_sum


def final_kernel(mean_ref, norm_in_ref, x_ref, centroids_ref, penalty_ref, out_ref, energy_ref, bias_ref, norm_ref):
    parts = norm_in_ref.shape[0]
    mean_sq = mean_ref[0, 0]
    factor = LOG2E * 2.0 / (sharpness * mean_ref[0:1, :])
    factor = jnp.concatenate([factor, factor], axis=1)
    fill_bias(mean_sq, centroids_ref, penalty_ref, bias_ref)
    log_sum = unpack_norms(norm_in_ref[...].reshape(parts, 128), norm_ref)
    energy_ref[...] = jnp.full(energy_ref.shape, -log_sum / (energy_scale * x_ref.shape[0] / CAP * 256), f32)
    slots = x_ref.shape[0]
    n, d = centroids_ref.shape
    kb = 256

    def block(b, _):
        rows = pl.ds(pl.multiple_of(b * kb, kb), kb)
        c = centroids_ref[rows, :]
        bias = wide(bias_ref, rows, 256)
        acc = jnp.zeros((kb, d), f32)
        mass = jnp.zeros((kb, 128), f32)
        for t in range(slots // 256):
            x = x_ref[t * 256 : (t + 1) * 256, :]
            norm = jnp.concatenate([norm_ref[2 * t], norm_ref[2 * t + 1]], axis=1)
            w = jnp.exp2((nt(c, x) - bias) * factor - norm).astype(bf16)
            acc = acc + jnp.dot(w, x, preferred_element_type=f32)
            w = w.astype(f32)
            mass = mass + w[:, :128] + w[:, 128:]
        mass = jnp.sum(mass, axis=1, keepdims=True)
        out_ref[rows, :] = (c.astype(f32) + acc) / (1.0 + mass)
        return 0

    lax.fori_loop(0, n // kb, block, 0)


def call(kernel, out_shape, scratch, *args):
    return pl.pallas_call(
        kernel,
        out_shape=out_shape,
        scratch_shapes=scratch,
        compiler_params=pltpu.CompilerParams(vmem_limit_bytes=56 * MIB),
    )(*args)


def exchange(x):
    return lax.all_to_all(x, AXES, split_axis=0, concat_axis=0, tiled=True)


def body(vectors, owners, centroids, penalty):
    rows, d = vectors.shape
    parts = lax.axis_size(AXES)
    n = centroids.shape[0]
    slots = parts * CAP
    shape = jax.ShapeDtypeStruct
    local_sq = jnp.sum(jnp.square(vectors.astype(f32)))
    all_sq = exchange(jnp.broadcast_to(local_sq, (parts, 1, 128)))
    mean_sq = jnp.sum(all_sq, axis=0) / (rows * parts * d)
    sq = jnp.broadcast_to(local_sq, (1, 128))
    penalty = penalty.reshape(n // 128, 128)
    out, rank, src = call(
        arrange_kernel,
        (shape((slots, d), bf16), shape((parts, rows), i32), shape((parts, 128), i32)),
        [],
        owners,
        vectors,
    )
    x = exchange(out.reshape(parts, CAP, d)).reshape(slots, d)
    lse = call(
        stats_kernel,
        shape((parts, 1, 128), f32),
        [pltpu.VMEM((n, 128), f32), pltpu.VMEM((n, 256), f32)],
        mean_sq,
        x,
        centroids,
        penalty,
    )
    norm = call(home_kernel, shape((parts, 1, 128), f32), [], mean_sq, sq, exchange(lse), rank, src)
    refined, energy = call(
        final_kernel,
        (shape((n, d), f32), shape((1, 128), f32)),
        [pltpu.VMEM((n, 128), f32), pltpu.VMEM((slots // 128, 1, 128), f32)],
        mean_sq,
        exchange(norm),
        x,
        centroids,
        penalty,
    )
    return refined, energy[0, 0]


def solution(mesh):
    placed = (P(AXES, None), P(AXES, None), P(AXES, None), P(AXES))
    return jax.shard_map(
        body, mesh=mesh, in_specs=placed, out_specs=(P(AXES, None), P()), check_vma=False
    )
```

time: 370 us -> 126 us (0.34)
  blocking collectives: 149 us -> 30.7 us
  matrix products: 69.5 us -> 0 us
  local copies, waits for them, and re-layouts: 74 us -> 5.26 us
  Pallas kernels: 0 us -> 37 us
  starting transfers between devices: 41.6 us -> 16.8 us
  waiting for transfers between devices: 8.89 us -> 33.3 us
  other arithmetic: 21.8 us -> 2.2 us
    psum x2 -> x0, blocking collectives: 149 us -> none  [the longest x1 81.2 us: body(): total_sq = lax.psum(local_sq, ('dp', 'cent'))]
    dot_general x24 -> x0, matrix products: 69.5 us -> none  [the longest x16 44.2 us: logits_for(): lax.dot_general(row_block, centroids, (((1,), (1,)), ((), ())), preferred...]
    unnamed x19 -> x3, local copies, waits for them, and re-layouts: 40.8 us -> 2.81 us
    pallas_call x0 -> x4, Pallas kernels: none -> 37 us  [call(): pl.pallas_call(kernel, out_shape=out_shape, scratch_shapes=scratch, compi...]
    all_to_all x0 -> x2, blocking collectives: none -> 30.7 us  [exchange(): return lax.all_to_all(x, AXES, split_axis=0, concat_axis=0, tiled=True)]
    gather x2 -> x0, local copies, waits for them, and re-layouts: 27.2 us -> none  [the longest x1 13.6 us: body(): slot_peak = back_peak[targets, position].reshape(row_count, replicas)]
    all_to_all x5 -> x2, starting transfers between devices: 41.6 us -> 16.8 us  [exchange(): return lax.all_to_all(x, AXES, split_axis=0, concat_axis=0, tiled=True)]
    all_to_all x5 -> x2, waiting for transfers between devices: 8.89 us -> 33.3 us  [exchange(): return lax.all_to_all(x, AXES, split_axis=0, concat_axis=0, tiled=True)]
  transfers between devices with their start and end apart: 5 -> 2, of which waited for: 1 -> 2; matrix products, arithmetic and copies ran while one was open for 15% -> 2% of each run, Pallas kernels for 0% -> 3%
where the time goes in v1:
time: 126 us
  Pallas kernels  37 us (29%)
  waiting for transfers between devices  33.3 us (26%)
  blocking collectives  30.7 us (24%)
  starting transfers between devices  16.8 us (13%)
  local copies, waits for them, and re-layouts  5.26 us (4%)
  other arithmetic  2.2 us (2%)
    pallas_call x4, Pallas kernels, call(): pl.pallas_call(kernel, out_shape=out_shape, scratch_shapes=scratch, compi...  37 us
    all_to_all x2, waiting for transfers between devices, exchange(): return lax.all_to_all(x, AXES, split_axis=0, concat_axis=0, tiled=True)  33.3 us
    all_to_all x2, blocking collectives, exchange(): return lax.all_to_all(x, AXES, split_axis=0, concat_axis=0, tiled=True)  30.7 us
    all_to_all x2, starting transfers between devices, exchange(): return lax.all_to_all(x, AXES, split_axis=0, concat_axis=0, tiled=True)  16.8 us
    unnamed x3, local copies, waits for them, and re-layouts  2.81 us
  transfers between devices with their start and end apart: 2, of which 2 were waited for; matrix products, arithmetic and copies ran while one was open for 2% of the time, Pallas kernels for 3%

profile of v1, /device:TPU:1, one launch (start us, length us, event | category | flops | bytes accessed | tf_op | source)
XLA Modules:
  0.0 125.9 jit_solution(7356261967538125600)
XLA Ops:
  0.6 1.6 %multiply_reduce_fusion = f32[]{:T(128)} fusion(bf16[256,256]{1,0:T(8,128)(2,1)} %vectors_ref.1), kind=kLoop, calls=%fused_computation | loop fusion | flops 196607 | bytes 131076 | tf_op jit(solution)/shard_map/reduce_sum | solution.py:206
  2.2 1.3 %broadcast_in_dim.6 = f32[128,1,128]{2,1,0:T(1,128)} broadcast(f32[]{:T(128)} %multiply_reduce_fusion), dimensions={} | broadcast | bytes 65540 | tf_op jit(solution)/shard_map/broadcast_in_dim | solution.py:207
  3.5 11.5 %all-to-all-start = ((f32[128,1,128]{2,1,0:T(1,128)}), f32[128,1,128]{2,1,0:T(1,128)S(1)}, u32[]{:S(2)}, u32[]{:S(2)}) async-start(f32[128,1,128]{2,1,0:T(1,128)} %broadcast_in_dim.6), calls=%async_computation | async-start | bytes 131072 | tf_op jit(solution)/shard_map/all_to_all | solution.py:197
  15.0 1.5 %copy.9.owners_ref = s32[256,8]{1,0:T(8,128)} copy(s32[256,8]{0,1:T(8,128)} %param.5) | data formatting | bytes 16384 | tf_op args[1]
  16.5 3.7 %shard_map.59 = (bf16[4096,256]{1,0:T(8,128)(2,1)}, s32[128,256]{1,0:T(8,128)}, s32[128,128]{1,0:T(8,128)}) custom-call(s32[256,8]{1,0:T(8,128)} %copy.9.owners_ref, bf16[256,256]{1,0:T(8,128)(2,1)} %vectors_ref.1), custom_call_target="tpu_custom_call" | custom-call | tf_op jit(solution)/shard_map/pallas_call | solution.py:188
  20.1 4.4 %all-to-all-done = f32[128,1,128]{2,1,0:T(1,128)S(1)} async-done(((f32[128,1,128]{2,1,0:T(1,128)}), f32[128,1,128]{2,1,0:T(1,128)S(1)}, u32[]{:S(2)}, u32[]{:S(2)}) %all-to-all-start) | async-done | bytes 65568 | tf_op jit(solution)/shard_map/all_to_all | solution.py:197
  24.6 5.3 %all-to-all-start.1 = ((bf16[128,32,256]{2,1,0:T(8,128)(2,1)}), bf16[128,32,256]{2,1,0:T(8,128)(2,1)S(1)}, u32[]{:S(2)}, u32[]{:S(2)}) async-start(bf16[128,32,256]{2,1,0:T(8,128)(2,1)} %bitcast.10), calls=%async_computation.1 | async-start | bytes 4194304 | tf_op jit(solution)/shard_map/all_to_all | solution.py:197
  29.9 0.6 multiply_bitcast_fusion.mean_ref
  30.5 28.9 %all-to-all-done.1 = bf16[128,32,256]{2,1,0:T(8,128)(2,1)S(1)} async-done(((bf16[128,32,256]{2,1,0:T(8,128)(2,1)}), bf16[128,32,256]{2,1,0:T(8,128)(2,1)S(1)}, u32[]{:S(2)}, u32[]{:S(2)}) %all-to-all-start.1) | async-done | bytes 2097184 | tf_op jit(solution)/shard_map/all_to_all | solution.py:197
  59.4 0.0 copy-start
  59.4 1.3 %copy-done = bf16[128,32,256]{2,1,0:T(8,128)(2,1)} copy-done((bf16[128,32,256]{2,1,0:T(8,128)(2,1)}, bf16[128,32,256]{2,1,0:T(8,128)(2,1)S(1)}, u32[]{:S(2)}) %copy-start) | copy-done | bytes 2097176
  60.7 15.7 %shard_map.60 = f32[128,1,128]{2,1,0:T(1,128)} custom-call(f32[1,128]{1,0:T(1,128)} %multiply_bitcast_fusion.mean_ref, bf16[4096,256]{1,0:T(8,128)(2,1)} %bitcast.8, bf16[2048,256]{1,0:T(8,128)(2,1)} %centroids_ref.3, s32[16,128]{1,0:T(8,128)} %bitcast.12), custom_call_target="tpu_custom_call" | custom-call | tf_op jit(solution)/shard_map/pallas_call | solution.py:188
  76.4 15.4 %all_to_all.20.lse_ref = f32[128,1,128]{2,1,0:T(1,128)} all-to-all(f32[128,1,128]{2,1,0:T(1,128)} %shard_map.60), channel_id=1, replica_groups=mesh['dp'=8,'cent'=16] {'dp','cent'}, dimensions={0} | all-to-all | bytes 131072 | tf_op jit(solution)/shard_map/all_to_all | solution.py:197
  91.8 1.2 broadcast_in_dim.7.sq_ref
  93.0 2.0 %shard_map.61 = f32[128,1,128]{2,1,0:T(1,128)} custom-call(f32[1,128]{1,0:T(1,128)} %multiply_bitcast_fusion.mean_ref, f32[1,128]{1,0:T(1,128)} %broadcast_in_dim.7.sq_ref, f32[128,1,128]{2,1,0:T(1,128)} %all_to_all.20.lse_ref, s32[128,256]{1,0:T(8,128)} %get-tuple-element.8.rank_ref, s32[128,128]{1,0:T(8,128)} %get-tuple-element.9.src_ref), custom_call_target="tpu_custom_call" | custom-call | tf_op jit(solution)/shard_map/pallas_call | solution.py:188
  95.0 15.3 %all_to_all.21.norm_in_ref = f32[128,1,128]{2,1,0:T(1,128)} all-to-all(f32[128,1,128]{2,1,0:T(1,128)} %shard_map.61), channel_id=1, replica_groups=mesh['dp'=8,'cent'=16] {'dp','cent'}, dimensions={0} | all-to-all | bytes 131072 | tf_op jit(solution)/shard_map/all_to_all | solution.py:197
  110.2 15.7 %shard_map.62 = (f32[2048,256]{1,0:T(8,128)}, f32[1,128]{1,0:T(1,128)}) custom-call(f32[1,128]{1,0:T(1,128)} %multiply_bitcast_fusion.mean_ref, f32[128,1,128]{2,1,0:T(1,128)} %all_to_all.21.norm_in_ref, bf16[4096,256]{1,0:T(8,128)(2,1)} %bitcast.9, bf16[2048,256]{1,0:T(8,128)(2,1)} %centroids_ref.3, s32[16,128]{1,0:T(8,128)} %bitcast.13), custom_call_target="tpu_custom_call" | custom-call | tf_op jit(solution)/shard_map/pallas_call | solution.py:188
  (1 shorter events, 0.0 us)
Async XLA Ops:
  3.5 21.1 %all-to-all-start = ((f32[128,1,128]{2,1,0:T(1,128)}), f32[128,1,128]{2,1,0:T(1,128)S(1)}, u32[]{:S(2)}, u32[]{:S(2)}) async-start(f32[128,1,128]{2,1,0:T(1,128)} %broadcast_in_dim.6), calls=%async_computation | async-start | bytes 131072 | tf_op jit(solution)/shard_map/all_to_all | solution.py:197
  24.6 34.8 %all-to-all-start.1 = ((bf16[128,32,256]{2,1,0:T(8,128)(2,1)}), bf16[128,32,256]{2,1,0:T(8,128)(2,1)S(1)}, u32[]{:S(2)}, u32[]{:S(2)}) async-start(bf16[128,32,256]{2,1,0:T(8,128)(2,1)} %bitcast.10), calls=%async_computation.1 | async-start | bytes 4194304 | tf_op jit(solution)/shard_map/all_to_all | solution.py:197
  59.4 1.3 %copy-start = (bf16[128,32,256]{2,1,0:T(8,128)(2,1)}, bf16[128,32,256]{2,1,0:T(8,128)(2,1)S(1)}, u32[]{:S(2)}) copy-start(bf16[128,32,256]{2,1,0:T(8,128)(2,1)S(1)} %all-to-all-done.1) | copy-start | bytes 6291460

commit v2 on v1

v2 whole, which is shorter than its diff:
```python
import math

import jax
import jax.numpy as jnp
from jax import lax
from jax.experimental import pallas as pl
from jax.experimental.pallas import tpu as pltpu
from jax.sharding import PartitionSpec as P

sharpness = 4.0
penalty_weight = 0.5
energy_scale = 16.0

AXES = ("dp", "cent")
CAP = 32
DEAD = 3.0e38
LOG2E = math.log2(math.e)
LN2 = math.log(2.0)
MIB = 1024 * 1024

f32 = jnp.float32
bf16 = jnp.bfloat16
i32 = jnp.int32


def nt(a, b):
    return lax.dot_general(a, b, (((1,), (1,)), ((), ())), preferred_element_type=f32)


def iota(shape, axis):
    return lax.broadcasted_iota(i32, shape, axis)


PARTS = 128
INNER = 16
OUTER = 8
STRIDE = 37
GROUP = 8
LOGICAL = pl.DeviceIdType.LOGICAL


def jump(i):
    return lax.rem(i * STRIDE, PARTS)


def ahead(dp, cent, i):
    j = jump(i)
    return lax.rem(dp + j // INNER, OUTER) * INNER + lax.rem(cent + lax.rem(j, INNER), INNER)


def behind(dp, cent, i):
    j = jump(i)
    return lax.rem(dp + OUTER - j // INNER, OUTER) * INNER + lax.rem(cent + INNER - lax.rem(j, INNER), INNER)


def arrange(dp, cent, owners_t, vectors_ref, out_ref, rank_ref, src_ref):
    rows = vectors_ref.shape[0]
    step = iota((PARTS, rows), 0)
    j = jnp.bitwise_and(step * STRIDE, PARTS - 1)
    outer = jnp.bitwise_and(dp + jnp.right_shift(j, 4), OUTER - 1)
    part = outer * INNER + jnp.bitwise_and(cent + j, INNER - 1)
    match = part == owners_t[0:1, :]
    for r in range(1, owners_t.shape[0]):
        match = match | (part == owners_t[r : r + 1, :])
    before = jnp.where(iota((rows, rows), 0) < iota((rows, rows), 1), 1.0, 0.0).astype(bf16)
    rank = jnp.dot(jnp.where(match, 1.0, 0.0).astype(bf16), before, preferred_element_type=f32)
    rank_ref[...] = jnp.where(match, rank.astype(i32), -1)
    for g in range(PARTS // GROUP):
        ranks = rank_ref[g * GROUP : (g + 1) * GROUP, :]
        hot = ranks[:, None, :] == iota((GROUP, CAP, rows), 1)
        hot = jnp.where(hot, 1.0, 0.0).astype(bf16).reshape(GROUP * CAP, rows)
        picked = jnp.dot(hot, vectors_ref[...], preferred_element_type=f32).astype(bf16)
        out_ref[g * GROUP : (g + 1) * GROUP] = picked.reshape(GROUP, CAP, picked.shape[1])


def invert_ranks(rank_ref, src_ref):
    rows = rank_ref.shape[1]
    ranks = rank_ref[...]
    row = iota((PARTS, rows), 1)
    slot = iota((PARTS, 128), 1) - jnp.bitwise_and(iota((PARTS, 128), 0), 3) * CAP
    src = jnp.full((PARTS, 128), -1, i32)
    for j in range(CAP):
        here = jnp.max(jnp.where(ranks == j, row, -1), axis=1, keepdims=True)
        src = jnp.where(slot == j, here, src)
    src_ref[...] = src


def fill_bias(mean, centroids_ref, penalty_ref, bias_ref):
    n = centroids_ref.shape[0]
    eye = iota((128, 128), 0) == iota((128, 128), 1)
    for g in range(n // 128):
        c = centroids_ref[g * 128 : (g + 1) * 128, :].astype(f32)
        c = c * c
        half = sum(c[:, i : i + 128] for i in range(0, c.shape[1], 128)) * 0.5
        pen = penalty_ref[g : g + 1, :].astype(f32) * (penalty_weight * sharpness * 0.5) * mean
        col = jnp.sum(half + jnp.where(eye, pen, 0.0), axis=1, keepdims=True)
        bias_ref[g * 128 : (g + 1) * 128, :] = jnp.broadcast_to(col, (128, 128))


def chunk_stats(factor, x, t, centroids_ref, bias_ref, u_ref, kb):
    n = centroids_ref.shape[0]
    width = x.shape[0]
    peak = jnp.full((8, width), -DEAD, f32)
    for k in range(0, n, kb):
        b = bias_ref[k : k + kb, :]
        u = nt(centroids_ref[k : k + kb, :], x) - jnp.concatenate([b, b], axis=1)
        u_ref[t, k : k + kb, :] = u
        peak = jnp.maximum(peak, jnp.max(u.reshape(kb // 8, 8, width), axis=0))
    peak = jnp.max(peak, axis=0, keepdims=True)
    total = jnp.zeros((8, width), f32)
    for k in range(0, n, kb):
        p = jnp.exp2((u_ref[t, k : k + kb, :] - peak) * factor)
        total = total + jnp.sum(p.reshape(kb // 8, 8, width), axis=0)
    return peak * factor + jnp.log2(jnp.sum(total, axis=0, keepdims=True))


def home(mean, local_sq, lse, rank_ref, src_ref):
    rows = rank_ref.shape[1]
    quarter = jnp.bitwise_and(iota((PARTS, 128), 0), 3) * CAP
    logs = []
    for h in range(0, rows, 128):
        ranks = rank_ref[:, h : h + 128]
        live = ranks >= 0
        got = jnp.take_along_axis(lse, jnp.maximum(ranks, 0) + quarter, axis=1)
        peak = jnp.max(jnp.where(live, got, -DEAD), axis=0, keepdims=True)
        total = jnp.sum(jnp.where(live, jnp.exp2(got - peak), 0.0), axis=0, keepdims=True)
        logs.append(peak + jnp.log2(total))
    src = src_ref[...]
    norm = jnp.full((PARTS, 128), DEAD, f32)
    for h, log in enumerate(logs):
        got = jnp.take_along_axis(jnp.broadcast_to(log, (PARTS, 128)), jnp.bitwise_and(src, 127), axis=1)
        norm = jnp.where((src >= h * 128) & (src < (h + 1) * 128), got, norm)
    log_sum = LN2 * jnp.sum(sum(logs), axis=1, keepdims=True) - local_sq / (sharpness * mean)
    spare = jnp.bitwise_and(quarter + CAP, 127)
    return jnp.where(iota((PARTS, 128), 1) == spare, log_sum, norm)


def unpack_norms(dp, cent, norm, norm_ref):
    lane = iota((PARTS, 128), 1)
    j = jnp.bitwise_and(iota((PARTS, 128), 0) * STRIDE, PARTS - 1)
    outer = jnp.bitwise_and(dp + OUTER - jnp.right_shift(j, 4), OUTER - 1)
    sender = outer * INNER + jnp.bitwise_and(cent + PARTS - j, INNER - 1)
    quarter = jnp.bitwise_and(iota((PARTS, 128), 0), 3) * CAP
    spare = jnp.bitwise_and(quarter + CAP, 127)
    log_sum = jnp.sum(jnp.where(lane == spare, norm, 0.0), axis=1, keepdims=True)
    log_sum = jnp.sum(jnp.where(lane == sender, log_sum, 0.0), axis=0, keepdims=True)
    log_sum = jnp.sum(log_sum, axis=1, keepdims=True)
    mine = jnp.where(jnp.bitwise_and(lane, 96) == quarter, norm, 0.0)
    norm_ref[...] = jnp.sum(mine.reshape(PARTS // 4, 4, 128), axis=1)
    return log_sum


def kernel(
    owners_ref, vectors_ref, centroids_ref, penalty_ref, out_ref, energy_ref,
    send_ref, x_ref, u_ref, bias_ref, rank_ref, src_ref,
    sq_ref, outer_ref, inner_ref, lse_ref, lse_in_ref, norm_ref, norm_in_ref, norms_ref,
    x_out, x_in, sq_out, sq_in, lse_out, lse_in, norm_out, norm_in,
):
    dp, cent = lax.axis_index("dp"), lax.axis_index("cent")
    n, d = centroids_ref.shape
    rows = vectors_ref.shape[0]
    barrier = pltpu.get_barrier_semaphore()

    def greet(i, _):
        pl.semaphore_signal(barrier, inc=1, device_id=ahead(dp, cent, i), device_id_type=LOGICAL)
        return 0

    lax.fori_loop(1, PARTS, greet, 0)
    arrange(dp, cent, owners_ref[...].T, vectors_ref, send_ref, rank_ref, src_ref)
    x_ref[0] = send_ref[0]
    v = vectors_ref[...].astype(f32)
    local_sq = jnp.sum(jnp.sum(v * v, axis=0, keepdims=True), axis=1, keepdims=True)
    sq_ref[0] = jnp.broadcast_to(local_sq, (1, 128))
    outer_ref[0] = sq_ref[0]
    pl.semaphore_wait(barrier, PARTS - 1)

    def copy(src, dst, out_sem, in_sem, device):
        return pltpu.make_async_remote_copy(
            src_ref=src, dst_ref=dst, send_sem=out_sem, recv_sem=in_sem, device_id=device, device_id_type=LOGICAL
        )

    def wait_bytes(ref, sem):
        pltpu.make_async_copy(ref, ref, sem).wait()

    for i in range(1, OUTER):
        device = lax.rem(dp + i, OUTER) * INNER + cent
        copy(sq_ref.at[0], outer_ref.at[i], sq_out.at[0], sq_in.at[0], device).start()

    def send(i, _):
        copy(send_ref.at[i], x_ref.at[i], x_out, x_in.at[i // GROUP], ahead(dp, cent, i)).start()
        return 0

    lax.fori_loop(1, PARTS, send, 0)
    wait_bytes(outer_ref.at[pl.ds(1, OUTER - 1)], sq_in.at[0])
    sq_ref[1] = jnp.sum(outer_ref[...], axis=0)
    inner_ref[0] = sq_ref[1]
    for i in range(1, INNER):
        device = dp * INNER + lax.rem(cent + i, INNER)
        copy(sq_ref.at[1], inner_ref.at[i], sq_out.at[1], sq_in.at[1], device).start()
    invert_ranks(rank_ref, src_ref)
    wait_bytes(inner_ref.at[pl.ds(1, INNER - 1)], sq_in.at[1])
    mean = jnp.sum(inner_ref[...], axis=0) * (1.0 / (rows * PARTS * d))
    fill_bias(mean, centroids_ref, penalty_ref, bias_ref)
    factor = LOG2E * 2.0 / (sharpness * mean)
    factor = jnp.concatenate([factor, factor], axis=1)

    def send_lse(i, _):
        copy(lse_ref.at[i // 4], lse_in_ref.at[i], lse_out, lse_in, behind(dp, cent, i)).start()
        return 0

    def chunk(t):
        x = x_ref[pl.ds(t * GROUP, GROUP)].reshape(GROUP * CAP, d)
        lse = chunk_stats(factor, x, t, centroids_ref, bias_ref, u_ref, 256)
        lse_ref[2 * t] = lse[:, :128]
        lse_ref[2 * t + 1] = lse[:, 128:]

    wait_bytes(x_ref.at[pl.ds(1, GROUP - 1)], x_in.at[0])
    chunk(0)
    lse_in_ref[0] = lse_ref[0]
    lax.fori_loop(1, GROUP, send_lse, 0)

    def later(t, _):
        wait_bytes(x_ref.at[pl.ds(t * GROUP, GROUP)], x_in.at[t])
        chunk(t)
        lax.fori_loop(t * GROUP, (t + 1) * GROUP, send_lse, 0)
        return 0

    lax.fori_loop(1, PARTS // GROUP, later, 0)
    wait_bytes(lse_in_ref.at[pl.ds(1, PARTS - 1)], lse_in)
    norm = home(mean[:, 0:1], local_sq, lse_in_ref[...].reshape(PARTS, 128), rank_ref, src_ref)
    norm_ref[...] = norm.reshape(norm_ref.shape)
    norm_in_ref[0] = norm_ref[0]

    def send_norm(i, _):
        copy(norm_ref.at[i], norm_in_ref.at[i], norm_out, norm_in, ahead(dp, cent, i)).start()
        return 0

    lax.fori_loop(1, PARTS, send_norm, 0)
    wait_bytes(norm_in_ref.at[pl.ds(1, PARTS - 1)], norm_in)
    log_sum = unpack_norms(dp, cent, norm_in_ref[...].reshape(PARTS, 128), norms_ref)
    energy_ref[...] = jnp.broadcast_to(log_sum * (-1.0 / (energy_scale * rows * PARTS)), energy_ref.shape)
    kb = 256

    def block(b, _):
        ks = pl.ds(pl.multiple_of(b * kb, kb), kb)
        acc = jnp.zeros((kb, d), f32)
        mass = jnp.zeros((kb, 128), f32)
        for t in range(PARTS // GROUP):
            x = x_ref[t * GROUP : (t + 1) * GROUP].reshape(GROUP * CAP, d)
            log = jnp.concatenate([norms_ref[2 * t : 2 * t + 1, :], norms_ref[2 * t + 1 : 2 * t + 2, :]], axis=1)
            w = jnp.exp2(u_ref[t, ks, :] * factor - log).astype(bf16)
            acc = acc + jnp.dot(w, x, preferred_element_type=f32)
            w = w.astype(f32)
            mass = mass + w[:, :128] + w[:, 128:]
        mass = jnp.sum(mass, axis=1, keepdims=True)
        out_ref[ks, :] = (centroids_ref[ks, :].astype(f32) + acc) / (1.0 + mass)
        return 0

    lax.fori_loop(0, n // kb, block, 0)
    wait_bytes(x_ref.at[pl.ds(1, PARTS - 1)], x_out)
    wait_bytes(outer_ref.at[pl.ds(1, OUTER - 1)], sq_out.at[0])
    wait_bytes(inner_ref.at[pl.ds(1, INNER - 1)], sq_out.at[1])
    wait_bytes(lse_in_ref.at[pl.ds(1, PARTS - 1)], lse_out)
    wait_bytes(norm_in_ref.at[pl.ds(1, PARTS - 1)], norm_out)


def body(vectors, owners, centroids, penalty):
    rows, d = vectors.shape
    n = centroids.shape[0]
    shape = jax.ShapeDtypeStruct
    dma = pltpu.SemaphoreType.DMA
    line = (1, 128)
    refined, energy = pl.pallas_call(
        kernel,
        out_shape=(shape((n, d), f32), shape(line, f32)),
        scratch_shapes=[
            pltpu.VMEM((PARTS, CAP, d), bf16),
            pltpu.VMEM((PARTS, CAP, d), bf16),
            pltpu.VMEM((PARTS // GROUP, n, GROUP * CAP), f32),
            pltpu.VMEM((n, 128), f32),
            pltpu.VMEM((PARTS, rows), i32),
            pltpu.VMEM((PARTS, 128), i32),
            pltpu.VMEM((2,) + line, f32),
            pltpu.VMEM((OUTER,) + line, f32),
            pltpu.VMEM((INNER,) + line, f32),
            pltpu.VMEM((PARTS // 4,) + line, f32),
            pltpu.VMEM((PARTS,) + line, f32),
            pltpu.VMEM((PARTS,) + line, f32),
            pltpu.VMEM((PARTS,) + line, f32),
            pltpu.VMEM((PARTS // 4, 128), f32),
            dma,
            dma((PARTS // GROUP,)),
            dma((2,)),
            dma((2,)),
            dma,
            dma,
            dma,
            dma,
        ],
        compiler_params=pltpu.CompilerParams(
            collective_id=0, has_side_effects=True, vmem_limit_bytes=56 * MIB
        ),
    )(owners, vectors, centroids, penalty.reshape(n // 128, 128))
    return refined, energy[0, 0]


def solution(mesh):
    placed = (P(AXES, None), P(AXES, None), P(AXES, None), P(AXES))
    return jax.shard_map(
        body, mesh=mesh, in_specs=placed, out_specs=(P(AXES, None), P()), check_vma=False
    )
```

time: 126 us -> 84.9 us (0.67)
  Pallas kernels: 37 us -> 78.4 us
  waiting for transfers between devices: 33.3 us -> 0 us
  blocking collectives: 30.7 us -> 0 us
  starting transfers between devices: 16.8 us -> 0 us
  other arithmetic: 2.2 us -> 0 us
    pallas_call x4 -> x1, Pallas kernels: 37 us -> 78.4 us  [body(): pl.pallas_call(kernel, out_shape=(shape((n, d), f32), shape(line, f32)),...]
    all_to_all x2 -> x0, waiting for transfers between devices: 33.3 us -> none  [exchange(): return lax.all_to_all(x, AXES, split_axis=0, concat_axis=0, tiled=True)]
    all_to_all x2 -> x0, blocking collectives: 30.7 us -> none  [exchange(): return lax.all_to_all(x, AXES, split_axis=0, concat_axis=0, tiled=True)]
    all_to_all x2 -> x0, starting transfers between devices: 16.8 us -> none  [exchange(): return lax.all_to_all(x, AXES, split_axis=0, concat_axis=0, tiled=True)]
    broadcast_in_dim x2 -> x0, local copies, waits for them, and re-layouts: 2.45 us -> none  [the longest x1 1.3 us: body(): all_sq = exchange(jnp.broadcast_to(local_sq, (parts, 1, 128)))]
    unnamed x3 -> x4, local copies, waits for them, and re-layouts: 2.81 us -> 4.53 us
    reduce_sum x2 -> x0, other arithmetic: 1.61 us -> none  [the longest x1 1.58 us: body(): local_sq = jnp.sum(jnp.square(vectors.astype(f32)))]
  transfers between devices with their start and end apart: 2 -> 0, of which waited for: 2 -> 0; matrix products, arithmetic and copies ran while one was open for 2% -> 0% of each run, Pallas kernels for 3% -> 0%
where the time goes in v2:
time: 84.9 us; the launch traced here: 84.7 us
  Pallas kernels  78.4 us (92%)
  local copies, waits for them, and re-layouts  4.53 us (5%)
  between operations  1.81 us (2%)
    pallas_call x1, Pallas kernels, body(): pl.pallas_call(kernel, out_shape=(shape((n, d), f32), shape(line, f32)),...  78.4 us
    unnamed x4, local copies, waits for them, and re-layouts  4.53 us

profile of v2, /device:TPU:1, one launch (start us, length us, event | category | flops | bytes accessed | tf_op | source)
XLA Modules:
  0.0 84.7 jit_solution(3798057830215055510)
XLA Ops:
  0.6 1.5 %copy.6.owners_ref = s32[256,8]{1,0:T(8,128)} copy(s32[256,8]{0,1:T(8,128)} %param.5) | data formatting | bytes 16384 | tf_op args[1]
  2.1 78.4 %shard_map.59 = (f32[2048,256]{1,0:T(8,128)}, f32[1,128]{1,0:T(1,128)}) custom-call(s32[256,8]{1,0:T(8,128)} %copy.6.owners_ref, bf16[256,256]{1,0:T(8,128)(2,1)} %vectors_ref.1, bf16[2048,256]{1,0:T(8,128)(2,1)} %centroids_ref.1, s32[16,128]{1,0:T(8,128)} %bitcast.3), custom_call_target="tpu_custom_call" | custom-call | tf_op jit(solution)/shard_map/pallas_call | solution.py:273
  80.5 0.0 copy-start
  80.5 3.0 %copy.9 = f32[2048,256]{1,0:T(8,128)} copy(f32[2048,256]{1,0:T(8,128)} %get-tuple-element.8) | data formatting | bytes 4194304
  83.5 0.0 copy-done
Async XLA Ops:
  80.5 3.1 %copy-start = (f32[1,128]{1,0:T(1,128)S(1)}, f32[1,128]{1,0:T(1,128)}, u32[]{:S(2)}) copy-start(f32[1,128]{1,0:T(1,128)} %get-tuple-element.5) | copy-start | bytes 1540

commit v3 on v2

--- a/solution.py
+++ b/solution.py
@@ -34,8 +34,10 @@
 PARTS = 128
 INNER = 16
 OUTER = 8
-STRIDE = 37
+STRIDE = 85
 GROUP = 8
+GROUPS = PARTS // GROUP
+AHEAD = 7
 LOGICAL = pl.DeviceIdType.LOGICAL
 
 
@@ -53,7 +55,7 @@
     return lax.rem(dp + OUTER - j // INNER, OUTER) * INNER + lax.rem(cent + INNER - lax.rem(j, INNER), INNER)
 
 
-def arrange(dp, cent, owners_t, vectors_ref, out_ref, rank_ref, src_ref):
+def arrange(greet, dp, cent, owners_t, vectors_ref, out_ref, rank_ref, src_ref):
     rows = vectors_ref.shape[0]
     step = iota((PARTS, rows), 0)
     j = jnp.bitwise_and(step * STRIDE, PARTS - 1)
@@ -66,6 +68,7 @@
     rank = jnp.dot(jnp.where(match, 1.0, 0.0).astype(bf16), before, preferred_element_type=f32)
     rank_ref[...] = jnp.where(match, rank.astype(i32), -1)
     for g in range(PARTS // GROUP):
+        greet(g)
         ranks = rank_ref[g * GROUP : (g + 1) * GROUP, :]
         hot = ranks[:, None, :] == iota((GROUP, CAP, rows), 1)
         hot = jnp.where(hot, 1.0, 0.0).astype(bf16).reshape(GROUP * CAP, rows)
@@ -135,7 +138,7 @@
     return jnp.where(iota((PARTS, 128), 1) == spare, log_sum, norm)
 
 
-def unpack_norms(dp, cent, norm, norm_ref):
+def sum_logs(dp, cent, norm):
     lane = iota((PARTS, 128), 1)
     j = jnp.bitwise_and(iota((PARTS, 128), 0) * STRIDE, PARTS - 1)
     outer = jnp.bitwise_and(dp + OUTER - jnp.right_shift(j, 4), OUTER - 1)
@@ -145,15 +148,21 @@
     log_sum = jnp.sum(jnp.where(lane == spare, norm, 0.0), axis=1, keepdims=True)
     log_sum = jnp.sum(jnp.where(lane == sender, log_sum, 0.0), axis=0, keepdims=True)
     log_sum = jnp.sum(log_sum, axis=1, keepdims=True)
-    mine = jnp.where(jnp.bitwise_and(lane, 96) == quarter, norm, 0.0)
-    norm_ref[...] = jnp.sum(mine.reshape(PARTS // 4, 4, 128), axis=1)
     return log_sum
+
+
+def unpack_norms(norm_in_ref, norms_ref, half):
+    count = PARTS // 2
+    norm = norm_in_ref[half * count : (half + 1) * count].reshape(count, 128)
+    quarter = jnp.bitwise_and(iota((count, 128), 0), 3) * CAP
+    mine = jnp.where(jnp.bitwise_and(iota((count, 128), 1), 96) == quarter, norm, 0.0)
+    norms_ref[half * count // 4 : (half + 1) * count // 4, :] = jnp.sum(mine.reshape(count // 4, 4, 128), axis=1)
 
 
 def kernel(
     owners_ref, vectors_ref, centroids_ref, penalty_ref, out_ref, energy_ref,
     send_ref, x_ref, u_ref, bias_ref, rank_ref, src_ref,
-    sq_ref, outer_ref, inner_ref, lse_ref, lse_in_ref, norm_ref, norm_in_ref, norms_ref,
+    sq_ref, outer_ref, inner_ref, lse_ref, lse_in_ref, norm_ref, norm_in_ref, norms_ref, mass_ref,
     x_out, x_in, sq_out, sq_in, lse_out, lse_in, norm_out, norm_in,
 ):
     dp, cent = lax.axis_index("dp"), lax.axis_index("cent")
@@ -161,12 +170,12 @@
     rows = vectors_ref.shape[0]
     barrier = pltpu.get_barrier_semaphore()
 
-    def greet(i, _):
-        pl.semaphore_signal(barrier, inc=1, device_id=ahead(dp, cent, i), device_id_type=LOGICAL)
-        return 0
-
-    lax.fori_loop(1, PARTS, greet, 0)
-    arrange(dp, cent, owners_ref[...].T, vectors_ref, send_ref, rank_ref, src_ref)
+    def greet(g):
+        for i in range(g * GROUP, (g + 1) * GROUP):
+            if i > 0:
+                pl.semaphore_signal(barrier, inc=1, device_id=ahead(dp, cent, i), device_id_type=LOGICAL)
+
+    arrange(greet, dp, cent, owners_ref[...], vectors_ref, send_ref, rank_ref, src_ref)
     x_ref[0] = send_ref[0]
     v = vectors_ref[...].astype(f32)
     local_sq = jnp.sum(jnp.sum(v * v, axis=0, keepdims=True), axis=1, keepdims=True)
@@ -186,11 +195,15 @@
         device = lax.rem(dp + i, OUTER) * INNER + cent
         copy(sq_ref.at[0], outer_ref.at[i], sq_out.at[0], sq_in.at[0], device).start()
 
-    def send(i, _):
-        copy(send_ref.at[i], x_ref.at[i], x_out, x_in.at[i // GROUP], ahead(dp, cent, i)).start()
-        return 0
-
-    lax.fori_loop(1, PARTS, send, 0)
+    def send_group(g):
+        for k in range(GROUP):
+            i = g * GROUP + k
+            if isinstance(g, int) and i == 0:
+                continue
+            copy(send_ref.at[i], x_ref.at[i], x_out.at[g], x_in.at[g], ahead(dp, cent, i)).start()
+
+    for g in range(AHEAD):
+        send_group(g)
     wait_bytes(outer_ref.at[pl.ds(1, OUTER - 1)], sq_in.at[0])
     sq_ref[1] = jnp.sum(outer_ref[...], axis=0)
     inner_ref[0] = sq_ref[1]
@@ -204,9 +217,12 @@
     factor = LOG2E * 2.0 / (sharpness * mean)
     factor = jnp.concatenate([factor, factor], axis=1)
 
-    def send_lse(i, _):
-        copy(lse_ref.at[i // 4], lse_in_ref.at[i], lse_out, lse_in, behind(dp, cent, i)).start()
-        return 0
+    def send_lse(t):
+        for k in range(GROUP):
+            i = t * GROUP + k
+            if isinstance(t, int) and i == 0:
+                continue
+            copy(lse_ref.at[t * 2 + k // 4], lse_in_ref.at[i], lse_out, lse_in, behind(dp, cent, i)).start()
 
     def chunk(t):
         x = x_ref[pl.ds(t * GROUP, GROUP)].reshape(GROUP * CAP, d)
@@ -214,50 +230,73 @@
         lse_ref[2 * t] = lse[:, :128]
         lse_ref[2 * t + 1] = lse[:, 128:]
 
+    wait_bytes(x_ref.at[pl.ds(1, GROUP - 1)], x_out.at[0])
+    send_group(AHEAD)
     wait_bytes(x_ref.at[pl.ds(1, GROUP - 1)], x_in.at[0])
     chunk(0)
     lse_in_ref[0] = lse_ref[0]
-    lax.fori_loop(1, GROUP, send_lse, 0)
+    send_lse(0)
 
     def later(t, _):
-        wait_bytes(x_ref.at[pl.ds(t * GROUP, GROUP)], x_in.at[t])
+        group = x_ref.at[pl.ds(t * GROUP, GROUP)]
+        wait_bytes(group, x_out.at[t])
+
+        @pl.when(t < GROUPS - AHEAD)
+        def _():
+            send_group(t + AHEAD)
+
+        wait_bytes(group, x_in.at[t])
         chunk(t)
-        lax.fori_loop(t * GROUP, (t + 1) * GROUP, send_lse, 0)
+        send_lse(t)
         return 0
 
-    lax.fori_loop(1, PARTS // GROUP, later, 0)
+    lax.fori_loop(1, GROUPS, later, 0)
     wait_bytes(lse_in_ref.at[pl.ds(1, PARTS - 1)], lse_in)
     norm = home(mean[:, 0:1], local_sq, lse_in_ref[...].reshape(PARTS, 128), rank_ref, src_ref)
     norm_ref[...] = norm.reshape(norm_ref.shape)
     norm_in_ref[0] = norm_ref[0]
 
-    def send_norm(i, _):
-        copy(norm_ref.at[i], norm_in_ref.at[i], norm_out, norm_in, ahead(dp, cent, i)).start()
-        return 0
-
-    lax.fori_loop(1, PARTS, send_norm, 0)
-    wait_bytes(norm_in_ref.at[pl.ds(1, PARTS - 1)], norm_in)
-    log_sum = unpack_norms(dp, cent, norm_in_ref[...].reshape(PARTS, 128), norms_ref)
+    def send_norm(half):
+        def one(i, _):
+            copy(norm_ref.at[i], norm_in_ref.at[i], norm_out, norm_in.at[half], ahead(dp, cent, i)).start()
+            return 0
+
+        return one
+
+    lax.fori_loop(1, PARTS // 2, send_norm(0), 0, unroll=4)
+    lax.fori_loop(PARTS // 2, PARTS, send_norm(1), 0, unroll=4)
+    kb = 256
+
+    def block(half):
+        def run(b, _):
+            ks = pl.ds(pl.multiple_of(b * kb, kb), kb)
+            acc = jnp.zeros((kb, d), f32)
+            mass = jnp.zeros((kb, 128), f32)
+            for t in range(half * GROUPS // 2, (half + 1) * GROUPS // 2):
+                x = x_ref[t * GROUP : (t + 1) * GROUP].reshape(GROUP * CAP, d)
+                log = jnp.concatenate([norms_ref[2 * t : 2 * t + 1, :], norms_ref[2 * t + 1 : 2 * t + 2, :]], axis=1)
+                w = jnp.exp2(u_ref[t, ks, :] * factor - log).astype(bf16)
+                acc = acc + jnp.dot(w, x, preferred_element_type=f32)
+                w = w.astype(f32)
+                mass = mass + w[:, :128] + w[:, 128:]
+            if half == 0:
+                out_ref[ks, :] = acc
+                mass_ref[ks, :] = mass
+            else:
+                mass = jnp.sum(mass + mass_ref[ks, :], axis=1, keepdims=True)
+                out_ref[ks, :] = (centroids_ref[ks, :].astype(f32) + (acc + out_ref[ks, :])) / (1.0 + mass)
+            return 0
+
+        return run
+
+    wait_bytes(norm_in_ref.at[pl.ds(1, PARTS // 2 - 1)], norm_in.at[0])
+    unpack_norms(norm_in_ref, norms_ref, 0)
+    lax.fori_loop(0, n // kb, block(0), 0)
+    wait_bytes(norm_in_ref.at[pl.ds(PARTS // 2, PARTS // 2)], norm_in.at[1])
+    unpack_norms(norm_in_ref, norms_ref, 1)
+    log_sum = sum_logs(dp, cent, norm_in_ref[...].reshape(PARTS, 128))
     energy_ref[...] = jnp.broadcast_to(log_sum * (-1.0 / (energy_scale * rows * PARTS)), energy_ref.shape)
-    kb = 256
-
-    def block(b, _):
-        ks = pl.ds(pl.multiple_of(b * kb, kb), kb)
-        acc = jnp.zeros((kb, d), f32)
-        mass = jnp.zeros((kb, 128), f32)
-        for t in range(PARTS // GROUP):
-            x = x_ref[t * GROUP : (t + 1) * GROUP].reshape(GROUP * CAP, d)
-            log = jnp.concatenate([norms_ref[2 * t : 2 * t + 1, :], norms_ref[2 * t + 1 : 2 * t + 2, :]], axis=1)
-            w = jnp.exp2(u_ref[t, ks, :] * factor - log).astype(bf16)
-            acc = acc + jnp.dot(w, x, preferred_element_type=f32)
-            w = w.astype(f32)
-            mass = mass + w[:, :128] + w[:, 128:]
-        mass = jnp.sum(mass, axis=1, keepdims=True)
-        out_ref[ks, :] = (centroids_ref[ks, :].astype(f32) + acc) / (1.0 + mass)
-        return 0
-
-    lax.fori_loop(0, n // kb, block, 0)
-    wait_bytes(x_ref.at[pl.ds(1, PARTS - 1)], x_out)
+    lax.fori_loop(0, n // kb, block(1), 0)
     wait_bytes(outer_ref.at[pl.ds(1, OUTER - 1)], sq_out.at[0])
     wait_bytes(inner_ref.at[pl.ds(1, INNER - 1)], sq_out.at[1])
     wait_bytes(lse_in_ref.at[pl.ds(1, PARTS - 1)], lse_out)
@@ -288,19 +327,20 @@
             pltpu.VMEM((PARTS,) + line, f32),
             pltpu.VMEM((PARTS,) + line, f32),
             pltpu.VMEM((PARTS // 4, 128), f32),
-            dma,
-            dma((PARTS // GROUP,)),
+            pltpu.VMEM((n, 128), f32),
+            dma((GROUPS,)),
+            dma((GROUPS,)),
             dma((2,)),
             dma((2,)),
             dma,
             dma,
             dma,
-            dma,
+            dma((2,)),
         ],
         compiler_params=pltpu.CompilerParams(
             collective_id=0, has_side_effects=True, vmem_limit_bytes=56 * MIB
         ),
-    )(owners, vectors, centroids, penalty.reshape(n // 128, 128))
+    )(owners.T, vectors, centroids, penalty.reshape(n // 128, 128))
     return refined, energy[0, 0]
 
 

time: 84.9 us -> 74.6 us (0.88)
  Pallas kernels: 78.4 us -> 69.5 us
  local copies, waits for them, and re-layouts: 4.53 us -> 3.05 us
    pallas_call x1, Pallas kernels: 78.4 us -> 69.5 us  [body(): pl.pallas_call(kernel, out_shape=(shape((n, d), f32), shape(line, f32)),...]
    unnamed x4 -> x3, local copies, waits for them, and re-layouts: 4.53 us -> 3.05 us
where the time goes in v3:
time: 74.6 us; the launch traced here: 74.4 us
  Pallas kernels  69.5 us (93%)
  local copies, waits for them, and re-layouts  3.05 us (4%)
  between operations  1.81 us (2%)
    pallas_call x1, Pallas kernels, body(): pl.pallas_call(kernel, out_shape=(shape((n, d), f32), shape(line, f32)),...  69.5 us
    unnamed x3, local copies, waits for them, and re-layouts  3.05 us

profile of v3, /device:TPU:1, one launch (start us, length us, event | category | flops | bytes accessed | tf_op | source)
XLA Modules:
  0.0 74.4 jit_solution(11069581117759503211)
XLA Ops:
  0.6 69.5 %shard_map.59 = (f32[2048,256]{1,0:T(8,128)}, f32[1,128]{1,0:T(1,128)}) custom-call(s32[8,256]{1,0:T(8,128)} %bitcast.4, bf16[256,256]{1,0:T(8,128)(2,1)} %vectors_ref.1, bf16[2048,256]{1,0:T(8,128)(2,1)} %centroids_ref.1, s32[16,128]{1,0:T(8,128)} %bitcast.5), custom_call_target="tpu_custom_call" | custom-call | tf_op jit(solution)/shard_map/pallas_call | solution.py:312
  70.1 0.0 copy-start
  70.2 3.0 %copy.8 = f32[2048,256]{1,0:T(8,128)} copy(f32[2048,256]{1,0:T(8,128)} %get-tuple-element.8) | data formatting | bytes 4194304
  73.2 0.0 copy-done
Async XLA Ops:
  70.1 3.1 %copy-start = (f32[1,128]{1,0:T(1,128)S(1)}, f32[1,128]{1,0:T(1,128)}, u32[]{:S(2)}) copy-start(f32[1,128]{1,0:T(1,128)} %get-tuple-element.5) | copy-start | bytes 1540

commit v4 on v3

--- a/solution.py
+++ b/solution.py
@@ -113,8 +113,10 @@
     total = jnp.zeros((8, width), f32)
     for k in range(0, n, kb):
         p = jnp.exp2((u_ref[t, k : k + kb, :] - peak) * factor)
+        u_ref[t, k : k + kb, :] = p
         total = total + jnp.sum(p.reshape(kb // 8, 8, width), axis=0)
-    return peak * factor + jnp.log2(jnp.sum(total, axis=0, keepdims=True))
+    peak = peak * factor
+    return peak, peak + jnp.log2(jnp.sum(total, axis=0, keepdims=True))
 
 
 def home(mean, local_sq, lse, rank_ref, src_ref):
@@ -151,18 +153,21 @@
     return log_sum
 
 
-def unpack_norms(norm_in_ref, norms_ref, half):
+def unpack_norms(norm_in_ref, norms_ref, peak_ref, half):
     count = PARTS // 2
     norm = norm_in_ref[half * count : (half + 1) * count].reshape(count, 128)
     quarter = jnp.bitwise_and(iota((count, 128), 0), 3) * CAP
     mine = jnp.where(jnp.bitwise_and(iota((count, 128), 1), 96) == quarter, norm, 0.0)
     norms_ref[half * count // 4 : (half + 1) * count // 4, :] = jnp.sum(mine.reshape(count // 4, 4, 128), axis=1)
+    for t in range(half * GROUPS // 2, (half + 1) * GROUPS // 2):
+        norm = jnp.concatenate([norms_ref[2 * t : 2 * t + 1, :], norms_ref[2 * t + 1 : 2 * t + 2, :]], axis=1)
+        peak_ref[t] = jnp.exp2(peak_ref[t] - norm)
 
 
 def kernel(
     owners_ref, vectors_ref, centroids_ref, penalty_ref, out_ref, energy_ref,
     send_ref, x_ref, u_ref, bias_ref, rank_ref, src_ref,
-    sq_ref, outer_ref, inner_ref, lse_ref, lse_in_ref, norm_ref, norm_in_ref, norms_ref, mass_ref,
+    sq_ref, outer_ref, inner_ref, lse_ref, lse_in_ref, norm_ref, norm_in_ref, norms_ref, mass_ref, peak_ref,
     x_out, x_in, sq_out, sq_in, lse_out, lse_in, norm_out, norm_in,
 ):
     dp, cent = lax.axis_index("dp"), lax.axis_index("cent")
@@ -226,7 +231,8 @@
 
     def chunk(t):
         x = x_ref[pl.ds(t * GROUP, GROUP)].reshape(GROUP * CAP, d)
-        lse = chunk_stats(factor, x, t, centroids_ref, bias_ref, u_ref, 256)
+        peak, lse = chunk_stats(factor, x, t, centroids_ref, bias_ref, u_ref, 256)
+        peak_ref[t] = peak
         lse_ref[2 * t] = lse[:, :128]
         lse_ref[2 * t + 1] = lse[:, 128:]
 
@@ -274,8 +280,7 @@
             mass = jnp.zeros((kb, 128), f32)
             for t in range(half * GROUPS // 2, (half + 1) * GROUPS // 2):
                 x = x_ref[t * GROUP : (t + 1) * GROUP].reshape(GROUP * CAP, d)
-                log = jnp.concatenate([norms_ref[2 * t : 2 * t + 1, :], norms_ref[2 * t + 1 : 2 * t + 2, :]], axis=1)
-                w = jnp.exp2(u_ref[t, ks, :] * factor - log).astype(bf16)
+                w = (u_ref[t, ks, :] * peak_ref[t]).astype(bf16)
                 acc = acc + jnp.dot(w, x, preferred_element_type=f32)
                 w = w.astype(f32)
                 mass = mass + w[:, :128] + w[:, 128:]
@@ -290,10 +295,10 @@
         return run
 
     wait_bytes(norm_in_ref.at[pl.ds(1, PARTS // 2 - 1)], norm_in.at[0])
-    unpack_norms(norm_in_ref, norms_ref, 0)
+    unpack_norms(norm_in_ref, norms_ref, peak_ref, 0)
     lax.fori_loop(0, n // kb, block(0), 0)
     wait_bytes(norm_in_ref.at[pl.ds(PARTS // 2, PARTS // 2)], norm_in.at[1])
-    unpack_norms(norm_in_ref, norms_ref, 1)
+    unpack_norms(norm_in_ref, norms_ref, peak_ref, 1)
     log_sum = sum_logs(dp, cent, norm_in_ref[...].reshape(PARTS, 128))
     energy_ref[...] = jnp.broadcast_to(log_sum * (-1.0 / (energy_scale * rows * PARTS)), energy_ref.shape)
     lax.fori_loop(0, n // kb, block(1), 0)
@@ -311,7 +316,7 @@
     line = (1, 128)
     refined, energy = pl.pallas_call(
         kernel,
-        out_shape=(shape((n, d), f32), shape(line, f32)),
+        out_shape=(pltpu.VMEM((n, d), f32), shape(line, f32)),
         scratch_shapes=[
             pltpu.VMEM((PARTS, CAP, d), bf16),
             pltpu.VMEM((PARTS, CAP, d), bf16),
@@ -328,6 +333,7 @@
             pltpu.VMEM((PARTS,) + line, f32),
             pltpu.VMEM((PARTS // 4, 128), f32),
             pltpu.VMEM((n, 128), f32),
+            pltpu.VMEM((GROUPS, 1, GROUP * CAP), f32),
             dma((GROUPS,)),
             dma((GROUPS,)),
             dma((2,)),
@@ -338,7 +344,7 @@
             dma((2,)),
         ],
         compiler_params=pltpu.CompilerParams(
-            collective_id=0, has_side_effects=True, vmem_limit_bytes=56 * MIB
+            collective_id=0, has_side_effects=True, vmem_limit_bytes=48 * MIB
         ),
     )(owners.T, vectors, centroids, penalty.reshape(n // 128, 128))
     return refined, energy[0, 0]

time: 74.6 us -> 73.4 us (0.984)
  Pallas kernels: 69.5 us -> 66.1 us
  local copies, waits for them, and re-layouts: 3.05 us -> 4.84 us
    pallas_call x1, Pallas kernels: 69.5 us -> 66.1 us  [body(): pl.pallas_call(kernel, out_shape=(pltpu.VMEM((n, d), f32), shape(line, f3...]
    unnamed x3 -> x9, local copies, waits for them, and re-layouts: 3.05 us -> 4.84 us
where the time goes in v4:
time: 73.4 us; the launch traced here: 72.8 us
  Pallas kernels  66.1 us (90%)
  local copies, waits for them, and re-layouts  4.84 us (7%)
  between operations  1.82 us (2%)
    pallas_call x1, Pallas kernels, body(): pl.pallas_call(kernel, out_shape=(pltpu.VMEM((n, d), f32), shape(line, f3...  66.1 us
    unnamed x9, local copies, waits for them, and re-layouts  4.84 us

profile of v4, /device:TPU:1, one launch (start us, length us, event | category | flops | bytes accessed | tf_op | source)
XLA Modules:
  0.0 72.8 jit_solution(10655965083083596293)
XLA Ops:
  0.6 0.0 copy-start
  0.6 1.2 %copy-done = bf16[2048,256]{1,0:T(8,128)(2,1)S(1)} copy-done((bf16[2048,256]{1,0:T(8,128)(2,1)S(1)}, bf16[2048,256]{1,0:T(8,128)(2,1)}, u32[]{:S(2)}) %copy-start) | copy-done | bytes 1048600
  1.9 0.0 copy-start.1
  1.9 0.9 %copy-done.1 = bf16[256,256]{1,0:T(8,128)(2,1)S(1)} copy-done((bf16[256,256]{1,0:T(8,128)(2,1)S(1)}, bf16[256,256]{1,0:T(8,128)(2,1)}, u32[]{:S(2)}) %copy-start.1) | copy-done | bytes 131096
  2.8 0.0 copy-start.2
  2.8 0.7 copy-done.2
  3.5 0.0 copy-start.3
  3.5 0.7 copy-done.3
  4.2 66.1 %shard_map.59 = (f32[2048,256]{1,0:T(8,128)S(1)}, f32[1,128]{1,0:T(1,128)S(1)}) custom-call(s32[8,256]{1,0:T(8,128)S(1)} %bitcast.4, bf16[256,256]{1,0:T(8,128)(2,1)S(1)} %copy-done.1, bf16[2048,256]{1,0:T(8,128)(2,1)S(1)} %copy-done, s32[16,128]{1,0:T(8,128)S(1)} %bitcast.5), custom_call_target="tpu_custom_call" | custom-call | tf_op jit(solution)/shard_map/pallas_call | solution.py:317
  70.3 1.3 %copy.8 = f32[2048,256]{1,0:T(8,128)} copy(f32[2048,256]{1,0:T(8,128)S(1)} %get-tuple-element.6) | data formatting | bytes 4194304
Async XLA Ops:
  0.6 1.2 %copy-start = (bf16[2048,256]{1,0:T(8,128)(2,1)S(1)}, bf16[2048,256]{1,0:T(8,128)(2,1)}, u32[]{:S(2)}) copy-start(bf16[2048,256]{1,0:T(8,128)(2,1)} %centroids_ref.1) | copy-start | bytes 3145732
  1.9 0.9 %copy-start.1 = (bf16[256,256]{1,0:T(8,128)(2,1)S(1)}, bf16[256,256]{1,0:T(8,128)(2,1)}, u32[]{:S(2)}) copy-start(bf16[256,256]{1,0:T(8,128)(2,1)} %vectors_ref.1) | copy-start | bytes 393220
  2.8 0.7 copy-start.2
  3.5 0.7 copy-start.3

commit v5 on v4

--- a/solution.py
+++ b/solution.py
@@ -269,8 +269,8 @@
 
         return one
 
-    lax.fori_loop(1, PARTS // 2, send_norm(0), 0, unroll=4)
-    lax.fori_loop(PARTS // 2, PARTS, send_norm(1), 0, unroll=4)
+    lax.fori_loop(1, PARTS // 2, send_norm(0), 0, unroll=True)
+    lax.fori_loop(PARTS // 2, PARTS, send_norm(1), 0, unroll=True)
     kb = 256
 
     def block(half):

time: 73.4 us -> 73.2 us (level)
  no operation moved by 1% of the time
where the time goes in v5:
time: 73.2 us; the launch traced here: 72.7 us
  Pallas kernels  66 us (90%)
  local copies, waits for them, and re-layouts  4.84 us (7%)
  between operations  1.82 us (2%)
    pallas_call x1, Pallas kernels, body(): pl.pallas_call(kernel, out_shape=(pltpu.VMEM((n, d), f32), shape(line, f3...  66 us
    unnamed x9, local copies, waits for them, and re-layouts  4.84 us

profile of v5, /device:TPU:1, one launch (start us, length us, event | category | flops | bytes accessed | tf_op | source)
XLA Modules:
  0.0 72.7 jit_solution(12623600558775006711)
XLA Ops:
  0.6 0.0 copy-start
  0.6 1.2 %copy-done = bf16[2048,256]{1,0:T(8,128)(2,1)S(1)} copy-done((bf16[2048,256]{1,0:T(8,128)(2,1)S(1)}, bf16[2048,256]{1,0:T(8,128)(2,1)}, u32[]{:S(2)}) %copy-start) | copy-done | bytes 1048600
  1.9 0.0 copy-start.1
  1.9 0.9 %copy-done.1 = bf16[256,256]{1,0:T(8,128)(2,1)S(1)} copy-done((bf16[256,256]{1,0:T(8,128)(2,1)S(1)}, bf16[256,256]{1,0:T(8,128)(2,1)}, u32[]{:S(2)}) %copy-start.1) | copy-done | bytes 131096
  2.8 0.0 copy-start.2
  2.8 0.7 copy-done.2
  3.5 0.0 copy-start.3
  3.5 0.7 copy-done.3
  4.2 66.0 %shard_map.59 = (f32[2048,256]{1,0:T(8,128)S(1)}, f32[1,128]{1,0:T(1,128)S(1)}) custom-call(s32[8,256]{1,0:T(8,128)S(1)} %bitcast.4, bf16[256,256]{1,0:T(8,128)(2,1)S(1)} %copy-done.1, bf16[2048,256]{1,0:T(8,128)(2,1)S(1)} %copy-done, s32[16,128]{1,0:T(8,128)S(1)} %bitcast.5), custom_call_target="tpu_custom_call" | custom-call | tf_op jit(solution)/shard_map/pallas_call | solution.py:317
  70.2 1.3 %copy.8 = f32[2048,256]{1,0:T(8,128)} copy(f32[2048,256]{1,0:T(8,128)S(1)} %get-tuple-element.6) | data formatting | bytes 4194304
Async XLA Ops:
  0.6 1.2 %copy-start = (bf16[2048,256]{1,0:T(8,128)(2,1)S(1)}, bf16[2048,256]{1,0:T(8,128)(2,1)}, u32[]{:S(2)}) copy-start(bf16[2048,256]{1,0:T(8,128)(2,1)} %centroids_ref.1) | copy-start | bytes 3145732
  1.9 0.9 %copy-start.1 = (bf16[256,256]{1,0:T(8,128)(2,1)S(1)}, bf16[256,256]{1,0:T(8,128)(2,1)}, u32[]{:S(2)}) copy-start(bf16[256,256]{1,0:T(8,128)(2,1)} %vectors_ref.1) | copy-start | bytes 393220
  2.8 0.7 copy-start.2
  3.5 0.7 copy-start.3
